TPU v7x, 32 devices: a whole 2x2x4 slice. The times are simulated.
32 devices in a mesh: rec: 2 (over y), leaf: 4 (over z), rhs: 2 (over x), pan: 2 (over core).
Axes of the slice: x: 2, y: 2, z: 4, core: 2. Of those that a mesh axis runs over, the one named last changes fastest.
Arguments:
- bottom_source: bfloat16 [32768, 256], P(('rec', 'leaf', 'rhs', 'pan')), parts along dimension 0, may hold values from -6 to 6
- bottom_inverse: bfloat16 [32768, 1024], P(('rec', 'leaf', 'rhs', 'pan')), parts along dimension 0, as said below
- bottom_update: bfloat16 [4096, 1024], P(('rec', 'leaf', 'rhs', 'pan')), parts along dimension 0, may hold values from -0.0625 to 0.0625
- bottom_sensitivity: bfloat16 [1024, 16384], P('rec', ('leaf', 'rhs', 'pan')), parts along dimension 0, may hold values from -0.03125 to 0.03125
- bottom_order: int32 [16, 1024], P(('leaf', 'rhs', 'pan')), may hold values from 0 to 1023, each once within a row
- bottom_extent: int32 [16], P(('leaf', 'rhs', 'pan')), may hold values from 384 to 1024, as said below
- bottom_targets: int32 [16, 128], P(('leaf', 'rhs', 'pan')), may hold values from 0 to 255, as said below
- upper_source: bfloat16 [3584, 256], P(('rec', 'leaf'), ('rhs', 'pan')), parts along dimension 0, may hold values from -6 to 6
- upper_inverse: bfloat16 [3584, 256], P(('rec', 'leaf')), parts along dimension 0, as said below
- upper_update: bfloat16 [256, 1536], P('rec', 'leaf'), parts along dimension 0, may hold values from -0.25 to 0.25
- upper_targets: int32 [6, 128], replicated, may hold values from 0 to 255, as said below
Outputs:
- adjoint: bfloat16 [32768, 256], P(('rec', 'leaf', 'rhs', 'pan')), parts along dimension 0
- gradient: float32 [1024, 256], P(('rec', 'leaf', 'rhs', 'pan')), parts along dimension 0
There are 2 independent parts, one for each index of `rec`. A program takes and returns all parts, laid end to end along the dimension named above; an argument that names none is the same for every part. Nothing has to cross between parts.
Inputs may be any that keep to these rules, and one draw needn't show every extreme that they name: `bottom_inverse`: lower triangular, with its diagonal between 0.6 and 1.4. `upper_inverse`: lower triangular in each front's row order, with its diagonal between 0.6 and 1.4. `bottom_extent`: a multiple of 128; some front uses all 1024 rows. `bottom_targets`: the rows of one front go to distinct rows. `upper_targets`: the rows of one front go to distinct rows.
All inputs are finite; a program needn't handle non-finite values.
Results may differ from a plain program's by a relative error of at most 0.0058.
Values may be sent and summed in bfloat16 or wider, within the bound.
A program may use at most 64 MiB of HBM per device.

v0:
```python
import jax
import jax.numpy as jnp
from jax import lax
from jax.sharding import PartitionSpec as P


def partner(value, axis, apart):
    mask = 2**apart
    pairs = [(source, source ^ mask) for source in range(lax.axis_size(axis))]
    return lax.ppermute(value, axis, pairs)


def climb_sum(values, bit_count):
    for bit_index in range(bit_count):
        values = values + partner(values, "leaf", bit_index)
    return values


def descend_sum(values, bit_count):
    for bit_index in range(bit_count):
        values = values + partner(values, "leaf", bit_index)
    return values


def shards(
    bottom_source,
    bottom_inverse,
    bottom_update,
    bottom_sensitivity,
    bottom_order,
    bottom_extent,
    bottom_targets,
    upper_source,
    upper_inverse,
    upper_update,
    upper_targets,
):
    leaves = lax.axis_size("leaf")
    depth = leaves.bit_length() - 1
    leaf_place = lax.axis_index("leaf")
    front_rows = bottom_inverse.shape[0]
    front_size = upper_inverse.shape[1]
    order_rows = bottom_order[0]
    row_mask = (jnp.arange(front_rows, dtype=jnp.int32) < bottom_extent[0]).astype(jnp.bfloat16)[
        :, None
    ]
    ordered = bottom_source[order_rows] * row_mask
    solved = (
        jnp.dot(bottom_inverse, ordered, preferred_element_type=jnp.float32) * row_mask
    ).astype(jnp.bfloat16)
    contrib = jnp.dot(bottom_update, solved, preferred_element_type=jnp.float32)
    spread = (
        jnp.zeros((front_size, contrib.shape[1]), jnp.float32).at[bottom_targets[0]].set(contrib)
    )
    summed = lax.psum(spread, ("rhs", "pan"))
    loads = lax.all_gather(upper_source, ("rhs", "pan"), axis=1, tiled=True)
    column_count = summed.shape[1]
    front_input = (loads[0:front_size].astype(jnp.float32) - summed).astype(jnp.bfloat16)
    solved_upper = []
    for height in range(depth + 1):
        row_count = front_size >> height
        offset = 2 * front_size - (2 * front_size >> height)
        inverse_now = upper_inverse[offset : offset + row_count]
        solved_front = jnp.dot(inverse_now, front_input, preferred_element_type=jnp.float32).astype(
            jnp.bfloat16
        )
        solved_upper.append(solved_front)
        if height < depth:
            update_now = upper_update[:, offset : offset + row_count]
            lifted = jnp.dot(update_now, solved_front, preferred_element_type=jnp.float32)
            map_row = 2 * leaves - (2 * leaves >> height) + leaf_place // (1 << height)
            targets = lax.dynamic_slice_in_dim(upper_targets, map_row, 1, 0)[0]
            partial_input = (
                jnp.zeros((front_size, column_count), jnp.float32).at[targets].set(-lifted)
            )
            parent_rows = front_size >> height + 1
            parent_offset = 2 * front_size - (2 * front_size >> height + 1)
            parent_place = leaf_place % (2 << height) * parent_rows
            own_load = loads[parent_offset : parent_offset + parent_rows].astype(jnp.float32)
            current = lax.dynamic_slice_in_dim(partial_input, parent_place, parent_rows, 0)
            partial_input = lax.dynamic_update_slice_in_dim(
                partial_input, current + own_load, parent_place, 0
            )
            front_input = climb_sum(partial_input, height + 1).astype(jnp.bfloat16)
    back_rows = None
    for height in range(depth, -1, -1):
        row_count = front_size >> height
        offset = 2 * front_size - (2 * front_size >> height)
        inverse_now = upper_inverse[offset : offset + row_count]
        if height == depth:
            residue = solved_upper[height]
        else:
            map_row = 2 * leaves - (2 * leaves >> height) + leaf_place // (1 << height)
            targets = lax.dynamic_slice_in_dim(upper_targets, map_row, 1, 0)[0]
            picked = back_rows[targets]
            update_now = upper_update[:, offset : offset + row_count]
            coupled = jnp.einsum(
                "rj,rc->jc", update_now, picked, preferred_element_type=jnp.float32
            )
            residue = (solved_upper[height].astype(jnp.float32) - coupled).astype(jnp.bfloat16)
        partial_back = jnp.einsum(
            "ij,ic->jc", inverse_now, residue, preferred_element_type=jnp.float32
        )
        back_rows = descend_sum(partial_back, height).astype(jnp.bfloat16)
    picked_root = back_rows[bottom_targets[0]]
    coupled_root = jnp.einsum(
        "rj,rc->jc", bottom_update, picked_root, preferred_element_type=jnp.float32
    )
    bottom_residue = ((solved.astype(jnp.float32) - coupled_root) * row_mask).astype(jnp.bfloat16)
    bottom_back = (
        jnp.einsum("ij,ic->jc", bottom_inverse, bottom_residue, preferred_element_type=jnp.float32)
        * row_mask
    ).astype(jnp.bfloat16)
    adjoint = jnp.zeros_like(bottom_back).at[order_rows].set(bottom_back)
    gradient = lax.psum_scatter(
        -jnp.dot(bottom_sensitivity, adjoint, preferred_element_type=jnp.float32),
        ("leaf", "rhs", "pan"),
        scatter_dimension=0,
        tiled=True,
    )
    return (adjoint, gradient)


def solution(mesh):
    placed = (
        P(("rec", "leaf", "rhs", "pan"), None),
        P(("rec", "leaf", "rhs", "pan"), None),
        P(("rec", "leaf", "rhs", "pan"), None),
        P("rec", ("leaf", "rhs", "pan")),
        P(("leaf", "rhs", "pan"), None),
        P(("leaf", "rhs", "pan")),
        P(("leaf", "rhs", "pan"), None),
        P(("rec", "leaf"), ("rhs", "pan")),
        P(("rec", "leaf"), None),
        P("rec", "leaf"),
        P(),
    )
    return jax.shard_map(
        shards,
        mesh=mesh,
        in_specs=placed,
        out_specs=(P(("rec", "leaf", "rhs", "pan"), None), P(("rec", "leaf", "rhs", "pan"), None)),
        check_vma=False,
    )
```

profile of v0, /device:TPU:0, one launch (start us, length us, event | category | flops | bytes accessed | tf_op | source)
XLA Modules:
  0.0 189.3 jit_solution(15696807839329698646)
XLA Ops:
  9.4 4.6 %gather_fusion = bf16[1024,256]{1,0:T(8,128)(2,1)S(1)} fusion(bf16[1024,256]{1,0:T(8,128)(2,1)} %param.11, s32[1024]{0:T(1024)S(1)} %broadcast_clamp_fusion), kind=kCustom, calls=%fused_computation | custom fusion | bytes 1052672 | tf_op jit(solution)/shard_map/gather | solution.py:47
  14.0 1.0 fusion.3
  15.0 0.8 copy-done.3
  16.2 1.7 scatter_custom_fusion
  18.0 7.2 %all_gather.3 = bf16[448,256]{0,1:T(8,128)(2,1)S(1)} all-gather(bf16[448,64]{0,1:T(8,128)(2,1)S(1)} %copy-done.7), channel_id=1, replica_groups=mesh['rec'=2,'leaf'=4,'rhs'=2,'pan'=2] {'rhs','pan'}, dimensions={1}, use_global_device_ids=true | all-gather | bytes 286720 | tf_op jit(solution)/shard_map/all_gather | solution.py:56
  25.5 0.8 fusion.45
  26.3 26.5 %all-reduce.2.cloned.1.call-done = f32[256,256]{1,0:T(8,128)} async-done(((f32[256,256]{1,0:T(8,128)}), f32[256,256]{1,0:T(8,128)}) %all-reduce.2.cloned.1.call-update) | async-done | bytes 262160 | tf_op jit(solution)/shard_map/psum | solution.py:55
  52.8 1.2 convolution_convert_fusion.1
  54.2 1.1 scatter_custom_fusion.1
  55.4 1.6 collective-permute-start
  57.0 5.1 %collective-permute-done = f32[256,256]{1,0:T(8,128)S(1)} collective-permute-done((f32[256,256]{1,0:T(8,128)S(1)}, f32[256,256]{1,0:T(8,128)S(1)}, u32[]{:S(2)}, u32[]{:S(2)}) %collective-permute-start) | collective-permute-done | bytes 262176 | tf_op jit(solution)/shard_map/ppermute | solution.py:10
  62.6 1.1 scatter_custom_fusion.2
  63.7 1.8 collective-permute-start.1
  65.5 4.6 %collective-permute-done.1 = f32[256,256]{1,0:T(8,128)S(1)} collective-permute-done((f32[256,256]{1,0:T(8,128)S(1)}, f32[256,256]{1,0:T(8,128)S(1)}, u32[]{:S(2)}, u32[]{:S(2)}) %collective-permute-start.1) | collective-permute-done | bytes 262176 | tf_op jit(solution)/shard_map/ppermute | solution.py:10
  70.2 3.3 %collective-permute-start.2 = (f32[256,256]{1,0:T(8,128)S(1)}, f32[256,256]{1,0:T(8,128)S(1)}, u32[]{:S(2)}, u32[]{:S(2)}) collective-permute-start(f32[256,256]{1,0:T(8,128)S(1)} %add.117), channel_id=1, source_target_pairs={{0,8},{4,12},{8,0},{12,4},{1,9},{5,13},{9,1},{13,5},{2,10},{6,14},... | collective-permute-start | bytes 786440 | tf_op jit(solution)/shard_map/ppermute | solution.py:10
  73.5 8.1 %collective-permute-done.2 = f32[256,256]{1,0:T(8,128)S(1)} collective-permute-done((f32[256,256]{1,0:T(8,128)S(1)}, f32[256,256]{1,0:T(8,128)S(1)}, u32[]{:S(2)}, u32[]{:S(2)}) %collective-permute-start.2) | collective-permute-done | bytes 262176 | tf_op jit(solution)/shard_map/ppermute | solution.py:10
  82.0 0.8 collective-permute-start.3
  82.8 5.6 %collective-permute-done.3 = f32[256,256]{0,1:T(8,128)S(1)} collective-permute-done((f32[256,256]{0,1:T(8,128)S(1)}, f32[256,256]{0,1:T(8,128)S(1)}, u32[]{:S(2)}, u32[]{:S(2)}) %collective-permute-start.3) | collective-permute-done | bytes 262176 | tf_op jit(solution)/shard_map/ppermute | solution.py:10
  88.5 2.8 %collective-permute-start.4 = (f32[256,256]{0,1:T(8,128)S(1)}, f32[256,256]{0,1:T(8,128)S(1)}, u32[]{:S(2)}, u32[]{:S(2)}) collective-permute-start(f32[256,256]{0,1:T(8,128)S(1)} %add.119), channel_id=1, source_target_pairs={{0,8},{4,12},{8,0},{12,4},{1,9},{5,13},{9,1},{13,5},{2,10},{6,14},... | collective-permute-start | bytes 786440 | tf_op jit(solution)/shard_map/ppermute | solution.py:10
  91.3 9.9 %collective-permute-done.4 = f32[256,256]{0,1:T(8,128)S(1)} collective-permute-done((f32[256,256]{0,1:T(8,128)S(1)}, f32[256,256]{0,1:T(8,128)S(1)}, u32[]{:S(2)}, u32[]{:S(2)}) %collective-permute-start.4) | collective-permute-done | bytes 262176 | tf_op jit(solution)/shard_map/ppermute | solution.py:10
  101.3 0.8 gather_fusion.1
  102.2 1.1 convolution_bitcast_fusion
  103.3 0.8 collective-permute-start.5
  104.1 6.5 %collective-permute-done.5 = f32[256,256]{0,1:T(8,128)S(1)} collective-permute-done((f32[256,256]{0,1:T(8,128)S(1)}, f32[256,256]{0,1:T(8,128)S(1)}, u32[]{:S(2)}, u32[]{:S(2)}) %collective-permute-start.5) | collective-permute-done | bytes 262176 | tf_op jit(solution)/shard_map/ppermute | solution.py:10
  110.8 0.8 gather_fusion.2
  111.6 1.2 fusion.7
  112.9 0.8 gather_fusion.3
  113.8 1.8 fusion.4
  115.8 5.1 %scatter_custom_fusion.3 = bf16[1024,256]{1,0:T(8,128)(2,1)S(1)} fusion(s32[1024]{0:T(1024)S(1)} %bitcast.59, bf16[1024,256]{1,0:T(8,128)(2,1)S(1)} %copy.36, bf16[]{:T(256)} %constant.56.clone.1), kind=kCustom, calls=%fused_computation.42 | custom fusion | bytes 524290 | tf_op jit(solution)/shard_map/scatter | solution.py:114
  120.9 1.9 %fusion.5 = f32[512,256]{0,1:T(8,128)S(1)} fusion(bf16[1024,256]{1,0:T(8,128)(2,1)S(1)} %scatter_custom_fusion.3, bf16[512,1024]{1,0:T(8,128)(2,1)} %param.14), kind=kOutput, calls=%fused_computation.17 | convolution fusion | flops 268566528 | bytes 2097152 | tf_op jit(solution)/shard_map/dot_general | solution.py:116
  122.8 1.0 copy.38
  123.9 58.6 %reduce-scatter.4.cloned.1.call-done = f32[32,256]{1,0:T(8,128)} async-done(((f32[512,256]{1,0:T(8,128)}), f32[32,256]{1,0:T(8,128)}) %reduce-scatter.4.cloned.1.call-update) | async-done | bytes 32784
  (50 shorter events, 4.1 us)
Async XLA Ops:
  7.2 6.8 %copy-start = (bf16[1024,1024]{1,0:T(8,128)(2,1)S(1)}, bf16[1024,1024]{1,0:T(8,128)(2,1)}, u32[]{:S(2)}) copy-start(bf16[1024,1024]{1,0:T(8,128)(2,1)} %param.12) | copy-start | bytes 6291460
  7.2 45.6 %all-reduce.2.cloned.1.call-start = ((), (), s32[]{:S(2)}) async-start(), calls=%async_computation.1 | async-start | bytes 524288 | tf_op jit(solution)/shard_map/psum | solution.py:55
  14.0 1.8 copy-start.6
  14.0 4.0 %copy-start.7 = (bf16[448,64]{0,1:T(8,128)(2,1)S(1)}, bf16[448,64]{0,1:T(8,128)(2,1)}, u32[]{:S(2)}) copy-start(bf16[448,64]{0,1:T(8,128)(2,1)} %param.18) | copy-start | bytes 172036
  15.0 0.8 copy-start.3
  15.8 36.9 %copy-start.2 = (bf16[448,256]{1,0:T(8,128)(2,1)S(1)}, bf16[448,256]{1,0:T(8,128)(2,1)}, u32[]{:S(2)}) copy-start(bf16[448,256]{1,0:T(8,128)(2,1)} %param.19) | copy-start | bytes 688132
  15.8 38.1 %copy-start.5 = (bf16[128,384]{1,0:T(8,128)(2,1)S(1)}, bf16[128,384]{1,0:T(8,128)(2,1)}, u32[]{:S(2)}) copy-start(bf16[128,384]{1,0:T(8,128)(2,1)} %param.20) | copy-start | bytes 294916
  17.9 164.5 %reduce-scatter.4.cloned.1.call-start = ((), (), s32[]{:S(2)}) async-start(), calls=%async_computation.2 | async-start | bytes 557056
  55.4 6.7 %collective-permute-start = (f32[256,256]{1,0:T(8,128)S(1)}, f32[256,256]{1,0:T(8,128)S(1)}, u32[]{:S(2)}, u32[]{:S(2)}) collective-permute-start(f32[256,256]{1,0:T(8,128)S(1)} %add_dynamic-update-slice_fusion), channel_id=1, source_target_pairs={{0,4},{4,0},{8,12},{12,8},{1,5},{5,1},{9,13},{13,9},{2,6},{6,2},{1... | collective-permute-start | bytes 786440 | tf_op jit(solution)/shard_map/ppermute | solution.py:10
  63.7 6.4 %collective-permute-start.1 = (f32[256,256]{1,0:T(8,128)S(1)}, f32[256,256]{1,0:T(8,128)S(1)}, u32[]{:S(2)}, u32[]{:S(2)}) collective-permute-start(f32[256,256]{1,0:T(8,128)S(1)} %add_dynamic-update-slice_fusion.1), channel_id=1, source_target_pairs={{0,4},{4,0},{8,12},{12,8},{1,5},{5,1},{9,13},{13,9},{2,6},{6,2},{1... | collective-permute-start | bytes 786440 | tf_op jit(solution)/shard_map/ppermute | solution.py:10
  70.2 11.4 %collective-permute-start.2 = (f32[256,256]{1,0:T(8,128)S(1)}, f32[256,256]{1,0:T(8,128)S(1)}, u32[]{:S(2)}, u32[]{:S(2)}) collective-permute-start(f32[256,256]{1,0:T(8,128)S(1)} %add.117), channel_id=1, source_target_pairs={{0,8},{4,12},{8,0},{12,4},{1,9},{5,13},{9,1},{13,5},{2,10},{6,14},... | collective-permute-start | bytes 786440 | tf_op jit(solution)/shard_map/ppermute | solution.py:10
  82.0 6.4 %collective-permute-start.3 = (f32[256,256]{0,1:T(8,128)S(1)}, f32[256,256]{0,1:T(8,128)S(1)}, u32[]{:S(2)}, u32[]{:S(2)}) collective-permute-start(f32[256,256]{0,1:T(8,128)S(1)} %convolution_bitcast_fusion.1), channel_id=1, source_target_pairs={{0,4},{4,0},{8,12},{12,8},{1,5},{5,1},{9,13},{13,9},{2,6},{6,2},{1... | collective-permute-start | bytes 786440 | tf_op jit(solution)/shard_map/ppermute | solution.py:10
  88.5 12.7 %collective-permute-start.4 = (f32[256,256]{0,1:T(8,128)S(1)}, f32[256,256]{0,1:T(8,128)S(1)}, u32[]{:S(2)}, u32[]{:S(2)}) collective-permute-start(f32[256,256]{0,1:T(8,128)S(1)} %add.119), channel_id=1, source_target_pairs={{0,8},{4,12},{8,0},{12,4},{1,9},{5,13},{9,1},{13,5},{2,10},{6,14},... | collective-permute-start | bytes 786440 | tf_op jit(solution)/shard_map/ppermute | solution.py:10
  101.2 12.6 %copy-start.4 = (bf16[256,1024]{1,0:T(8,128)(2,1)S(1)}, bf16[256,1024]{1,0:T(8,128)(2,1)}, u32[]{:S(2)}) copy-start(bf16[256,1024]{1,0:T(8,128)(2,1)} %copy-done.3) | copy-start | bytes 1572868
  103.3 7.3 %collective-permute-start.5 = (f32[256,256]{0,1:T(8,128)S(1)}, f32[256,256]{0,1:T(8,128)S(1)}, u32[]{:S(2)}, u32[]{:S(2)}) collective-permute-start(f32[256,256]{0,1:T(8,128)S(1)} %convolution_bitcast_fusion), channel_id=1, source_target_pairs={{0,4},{4,0},{8,12},{12,8},{1,5},{5,1},{9,13},{13,9},{2,6},{6,2},{1... | collective-permute-start | bytes 786440 | tf_op jit(solution)/shard_map/ppermute | solution.py:10
  120.9 61.5 %copy-start.1 = (bf16[1024,256]{1,0:T(8,128)(2,1)}, bf16[1024,256]{1,0:T(8,128)(2,1)S(1)}, u32[]{:S(2)}) copy-start(bf16[1024,256]{1,0:T(8,128)(2,1)S(1)} %scatter_custom_fusion.3) | copy-start | bytes 1572868
Sparse Core Ops, SparseCore 0:
  18.1 34.6 all-reduce.1
  124.0 58.4 reduce-scatter.3
where the time goes:
time: 190 us; the launch traced here: 189 us
  waiting for transfers between devices  125 us (66%)
  local copies, waits for them, and re-layouts  19 us (10%)
  between operations  15.2 us (8%)
  starting transfers between devices  11.1 us (6%)
  matrix products  9.46 us (5%)
  blocking collectives  7.19 us (4%)
  other arithmetic  2.34 us (1%)
    unnamed x3, waiting for transfers between devices  58.6 us
    ppermute x6, waiting for transfers between devices, partner(): return lax.ppermute(value, axis, pairs)  39.9 us
    psum x1, waiting for transfers between devices, shards(): summed = lax.psum(spread, ('rhs', 'pan'))  26.5 us
    ppermute x6, starting transfers between devices, partner(): return lax.ppermute(value, axis, pairs)  11 us
    all_gather x1, blocking collectives, shards(): loads = lax.all_gather(upper_source, ('rhs', 'pan'), axis=1, tiled=True)  7.19 us
    scatter x1, local copies, waits for them, and re-layouts, shards(): adjoint = jnp.zeros_like(bottom_back).at[order_rows].set(bottom_back)  5.07 us
    gather x1, local copies, waits for them, and re-layouts, shards(): ordered = bottom_source[order_rows] * row_mask  4.57 us
  transfers between devices with their start and end apart: 8, of which 8 were waited for; matrix products, arithmetic and copies ran while one was open for 1% of the time, Pallas kernels for 0%

commit v1 on v0

--- a/solution.py
+++ b/solution.py
@@ -52,7 +52,9 @@
     spread = (
         jnp.zeros((front_size, contrib.shape[1]), jnp.float32).at[bottom_targets[0]].set(contrib)
     )
-    summed = lax.psum(spread, ("rhs", "pan"))
+    summed = spread
+    for mesh_axis in ("pan", "rhs"):
+        summed = lax.psum(summed, mesh_axis)
     loads = lax.all_gather(upper_source, ("rhs", "pan"), axis=1, tiled=True)
     column_count = summed.shape[1]
     front_input = (loads[0:front_size].astype(jnp.float32) - summed).astype(jnp.bfloat16)

time: 190 us -> 205 us (1.079)
  waiting for transfers between devices: 125 us -> 143 us
    psum x1 -> x2, waiting for transfers between devices: 26.5 us -> 40.7 us  [shards(): summed = lax.psum(summed, mesh_axis)]
    ppermute x6, waiting for transfers between devices: 39.9 us -> 45.2 us  [partner(): return lax.ppermute(value, axis, pairs)]
    unnamed x3 -> x4, waiting for transfers between devices: 58.6 us -> 57 us
  transfers between devices with their start and end apart: 8 -> 9, of which waited for: 8 -> 9; matrix products, arithmetic and copies ran while one was open for 1% -> 1% of each run, Pallas kernels for 0% -> 0%
where the time goes in v1:
time: 205 us; the launch traced here: 204 us
  waiting for transfers between devices  143 us (70%)
  local copies, waits for them, and re-layouts  20 us (10%)
  between operations  14.9 us (7%)
  starting transfers between devices  9.57 us (5%)
  matrix products  8.66 us (4%)
  blocking collectives  5.98 us (3%)
  other arithmetic  2.35 us (1%)
    unnamed x4, waiting for transfers between devices  57 us
    ppermute x6, waiting for transfers between devices, partner(): return lax.ppermute(value, axis, pairs)  45.2 us
    psum x2, waiting for transfers between devices, shards(): summed = lax.psum(summed, mesh_axis)  40.7 us
    ppermute x6, starting transfers between devices, partner(): return lax.ppermute(value, axis, pairs)  9.45 us
    all_gather x1, blocking collectives, shards(): loads = lax.all_gather(upper_source, ('rhs', 'pan'), axis=1, tiled=True)  5.98 us
    scatter x1, local copies, waits for them, and re-layouts, shards(): adjoint = jnp.zeros_like(bottom_back).at[order_rows].set(bottom_back)  5.07 us
    gather x1, local copies, waits for them, and re-layouts, shards(): ordered = bottom_source[order_rows] * row_mask  4.57 us
  transfers between devices with their start and end apart: 9, of which 9 were waited for; matrix products, arithmetic and copies ran while one was open for 1% of the time, Pallas kernels for 0%

profile of v1, /device:TPU:0, one launch (start us, length us, event | category | flops | bytes accessed | tf_op | source)
XLA Modules:
  0.0 204.5 jit_solution(14554729601256036595)
XLA Ops:
  8.7 0.7 compare_select_fusion
  9.4 4.6 %gather_fusion = bf16[1024,256]{1,0:T(8,128)(2,1)S(1)} fusion(bf16[1024,256]{1,0:T(8,128)(2,1)} %param.11, s32[1024]{0:T(1024)S(1)} %broadcast_clamp_fusion), kind=kCustom, calls=%fused_computation | custom fusion | bytes 1052672 | tf_op jit(solution)/shard_map/gather | solution.py:47
  14.0 1.0 fusion.3
  15.0 0.8 copy-done.3
  16.2 1.7 scatter_custom_fusion
  18.0 21.1 %all-reduce.3.cloned.1.call-done = f32[256,256]{1,0:T(8,128)} async-done(((f32[256,256]{1,0:T(8,128)}), f32[256,256]{1,0:T(8,128)}) %all-reduce.3.cloned.1.call-update) | async-done | bytes 262160 | tf_op jit(solution)/shard_map/psum | solution.py:57
  39.1 6.0 %all_gather.3 = bf16[448,256]{0,1:T(8,128)(2,1)S(1)} all-gather(bf16[448,64]{0,1:T(8,128)(2,1)S(1)} %copy-done.7), channel_id=1, replica_groups=mesh['rec'=2,'leaf'=4,'rhs'=2,'pan'=2] {'rhs','pan'}, dimensions={1}, use_global_device_ids=true | all-gather | bytes 286720 | tf_op jit(solution)/shard_map/all_gather | solution.py:58
  45.4 0.8 fusion.45
  46.2 19.6 %all-reduce.5.cloned.1.call-done = f32[256,256]{1,0:T(8,128)} async-done(((f32[256,256]{1,0:T(8,128)}), f32[256,256]{1,0:T(8,128)}) %all-reduce.5.cloned.1.call-update) | async-done | bytes 262160 | tf_op jit(solution)/shard_map/psum | solution.py:57
  65.8 1.2 convolution_convert_fusion.1
  67.3 1.1 scatter_custom_fusion.1
  68.4 1.6 collective-permute-start
  70.1 6.0 %collective-permute-done = f32[256,256]{1,0:T(8,128)S(1)} collective-permute-done((f32[256,256]{1,0:T(8,128)S(1)}, f32[256,256]{1,0:T(8,128)S(1)}, u32[]{:S(2)}, u32[]{:S(2)}) %collective-permute-start) | collective-permute-done | bytes 262176 | tf_op jit(solution)/shard_map/ppermute | solution.py:10
  76.6 1.1 scatter_custom_fusion.2
  77.7 1.6 collective-permute-start.1
  79.2 5.2 %collective-permute-done.1 = f32[256,256]{1,0:T(8,128)S(1)} collective-permute-done((f32[256,256]{1,0:T(8,128)S(1)}, f32[256,256]{1,0:T(8,128)S(1)}, u32[]{:S(2)}, u32[]{:S(2)}) %collective-permute-start.1) | collective-permute-done | bytes 262176 | tf_op jit(solution)/shard_map/ppermute | solution.py:10
  84.5 2.5 %collective-permute-start.2 = (f32[256,256]{1,0:T(8,128)S(1)}, f32[256,256]{1,0:T(8,128)S(1)}, u32[]{:S(2)}, u32[]{:S(2)}) collective-permute-start(f32[256,256]{1,0:T(8,128)S(1)} %add.119), channel_id=1, source_target_pairs={{0,8},{4,12},{8,0},{12,4},{1,9},{5,13},{9,1},{13,5},{2,10},{6,14},... | collective-permute-start | bytes 786440 | tf_op jit(solution)/shard_map/ppermute | solution.py:10
  86.9 9.9 %collective-permute-done.2 = f32[256,256]{1,0:T(8,128)S(1)} collective-permute-done((f32[256,256]{1,0:T(8,128)S(1)}, f32[256,256]{1,0:T(8,128)S(1)}, u32[]{:S(2)}, u32[]{:S(2)}) %collective-permute-start.2) | collective-permute-done | bytes 262176 | tf_op jit(solution)/shard_map/ppermute | solution.py:10
  97.7 6.8 %collective-permute-done.3 = f32[256,256]{0,1:T(8,128)S(1)} collective-permute-done((f32[256,256]{0,1:T(8,128)S(1)}, f32[256,256]{0,1:T(8,128)S(1)}, u32[]{:S(2)}, u32[]{:S(2)}) %collective-permute-start.3) | collective-permute-done | bytes 262176 | tf_op jit(solution)/shard_map/ppermute | solution.py:10
  104.5 2.6 %collective-permute-start.4 = (f32[256,256]{0,1:T(8,128)S(1)}, f32[256,256]{0,1:T(8,128)S(1)}, u32[]{:S(2)}, u32[]{:S(2)}) collective-permute-start(f32[256,256]{0,1:T(8,128)S(1)} %add.121), channel_id=1, source_target_pairs={{0,8},{4,12},{8,0},{12,4},{1,9},{5,13},{9,1},{13,5},{2,10},{6,14},... | collective-permute-start | bytes 786440 | tf_op jit(solution)/shard_map/ppermute | solution.py:10
  107.1 10.9 %collective-permute-done.4 = f32[256,256]{0,1:T(8,128)S(1)} collective-permute-done((f32[256,256]{0,1:T(8,128)S(1)}, f32[256,256]{0,1:T(8,128)S(1)}, u32[]{:S(2)}, u32[]{:S(2)}) %collective-permute-start.4) | collective-permute-done | bytes 262176 | tf_op jit(solution)/shard_map/ppermute | solution.py:10
  118.1 0.8 gather_fusion.1
  119.3 0.8 collective-permute-start.5
  120.1 6.6 %collective-permute-done.5 = f32[256,256]{0,1:T(8,128)S(1)} collective-permute-done((f32[256,256]{0,1:T(8,128)S(1)}, f32[256,256]{0,1:T(8,128)S(1)}, u32[]{:S(2)}, u32[]{:S(2)}) %collective-permute-start.5) | collective-permute-done | bytes 262176 | tf_op jit(solution)/shard_map/ppermute | solution.py:10
  126.8 0.8 gather_fusion.2
  128.2 0.8 gather_fusion.3
  129.0 2.6 %fusion.4 = bf16[1024,256]{0,1:T(8,128)(2,1)} fusion(bf16[1024,1024]{1,0:T(8,128)(2,1)S(1)} %copy-done, bf16[128,256]{1,0:T(8,128)(2,1)S(1)} %gather_fusion.3, bf16[128,1024]{1,0:T(8,128)(2,1)} %param.13, bf16[256,1024]{1,0:T(8,128)(2,1)S(1)} %copy-done.4, f32[1024]{0:T(1024)S(1)} %get-tuple-element.11), kind=kOutput, calls=%fused_computation.15 | convolution fusion | flops 605552640 | bytes 3477504 | tf_op jit(solution)/shard_map/ij,ic->jc/dot_general | solution.py:113
  131.6 1.2 copy.36
  132.9 5.1 %scatter_custom_fusion.3 = bf16[1024,256]{1,0:T(8,128)(2,1)S(1)} fusion(s32[1024]{0:T(1024)S(1)} %bitcast.59, bf16[1024,256]{1,0:T(8,128)(2,1)S(1)} %copy.36, bf16[]{:T(256)} %constant.56.clone.1), kind=kCustom, calls=%fused_computation.42 | custom fusion | bytes 524290 | tf_op jit(solution)/shard_map/scatter | solution.py:116
  138.0 1.9 fusion.5
  139.9 1.0 copy.38
  140.9 57.0 %reduce-scatter.4.cloned.1.call-done = f32[32,256]{1,0:T(8,128)} async-done(((f32[512,256]{1,0:T(8,128)}), f32[32,256]{1,0:T(8,128)}) %reduce-scatter.4.cloned.1.call-update) | async-done | bytes 32784
  (53 shorter events, 4.5 us)
Async XLA Ops:
  7.2 6.8 %copy-start = (bf16[1024,1024]{1,0:T(8,128)(2,1)S(1)}, bf16[1024,1024]{1,0:T(8,128)(2,1)}, u32[]{:S(2)}) copy-start(bf16[1024,1024]{1,0:T(8,128)(2,1)} %param.12) | copy-start | bytes 6291460
  7.2 31.9 %all-reduce.3.cloned.1.call-start = ((), (), s32[]{:S(2)}) async-start(), calls=%async_computation.1 | async-start | bytes 524288 | tf_op jit(solution)/shard_map/psum | solution.py:57
  14.0 1.8 copy-start.6
  14.0 25.2 %copy-start.7 = (bf16[448,64]{0,1:T(8,128)(2,1)S(1)}, bf16[448,64]{0,1:T(8,128)(2,1)}, u32[]{:S(2)}) copy-start(bf16[448,64]{0,1:T(8,128)(2,1)} %param.18) | copy-start | bytes 172036
  15.0 0.8 copy-start.3
  15.8 50.0 %copy-start.2 = (bf16[448,256]{1,0:T(8,128)(2,1)S(1)}, bf16[448,256]{1,0:T(8,128)(2,1)}, u32[]{:S(2)}) copy-start(bf16[448,256]{1,0:T(8,128)(2,1)} %param.19) | copy-start | bytes 688132
  15.8 51.2 %copy-start.5 = (bf16[128,384]{1,0:T(8,128)(2,1)S(1)}, bf16[128,384]{1,0:T(8,128)(2,1)}, u32[]{:S(2)}) copy-start(bf16[128,384]{1,0:T(8,128)(2,1)} %param.20) | copy-start | bytes 294916
  17.9 47.9 %all-reduce.5.cloned.1.call-start = ((), (), s32[]{:S(2)}) async-start(), calls=%async_computation.2 | async-start | bytes 524288 | tf_op jit(solution)/shard_map/psum | solution.py:57
  39.1 158.8 %reduce-scatter.4.cloned.1.call-start = ((), (), s32[]{:S(2)}) async-start(), calls=%async_computation.3 | async-start | bytes 557056
  68.4 7.7 %collective-permute-start = (f32[256,256]{1,0:T(8,128)S(1)}, f32[256,256]{1,0:T(8,128)S(1)}, u32[]{:S(2)}, u32[]{:S(2)}) collective-permute-start(f32[256,256]{1,0:T(8,128)S(1)} %add_dynamic-update-slice_fusion), channel_id=1, source_target_pairs={{0,4},{4,0},{8,12},{12,8},{1,5},{5,1},{9,13},{13,9},{2,6},{6,2},{1... | collective-permute-start | bytes 786440 | tf_op jit(solution)/shard_map/ppermute | solution.py:10
  77.7 6.7 %collective-permute-start.1 = (f32[256,256]{1,0:T(8,128)S(1)}, f32[256,256]{1,0:T(8,128)S(1)}, u32[]{:S(2)}, u32[]{:S(2)}) collective-permute-start(f32[256,256]{1,0:T(8,128)S(1)} %add_dynamic-update-slice_fusion.1), channel_id=1, source_target_pairs={{0,4},{4,0},{8,12},{12,8},{1,5},{5,1},{9,13},{13,9},{2,6},{6,2},{1... | collective-permute-start | bytes 786440 | tf_op jit(solution)/shard_map/ppermute | solution.py:10
  84.5 12.3 %collective-permute-start.2 = (f32[256,256]{1,0:T(8,128)S(1)}, f32[256,256]{1,0:T(8,128)S(1)}, u32[]{:S(2)}, u32[]{:S(2)}) collective-permute-start(f32[256,256]{1,0:T(8,128)S(1)} %add.119), channel_id=1, source_target_pairs={{0,8},{4,12},{8,0},{12,4},{1,9},{5,13},{9,1},{13,5},{2,10},{6,14},... | collective-permute-start | bytes 786440 | tf_op jit(solution)/shard_map/ppermute | solution.py:10
  97.2 7.3 %collective-permute-start.3 = (f32[256,256]{0,1:T(8,128)S(1)}, f32[256,256]{0,1:T(8,128)S(1)}, u32[]{:S(2)}, u32[]{:S(2)}) collective-permute-start(f32[256,256]{0,1:T(8,128)S(1)} %convolution_bitcast_fusion.1), channel_id=1, source_target_pairs={{0,4},{4,0},{8,12},{12,8},{1,5},{5,1},{9,13},{13,9},{2,6},{6,2},{1... | collective-permute-start | bytes 786440 | tf_op jit(solution)/shard_map/ppermute | solution.py:10
  104.5 13.5 %collective-permute-start.4 = (f32[256,256]{0,1:T(8,128)S(1)}, f32[256,256]{0,1:T(8,128)S(1)}, u32[]{:S(2)}, u32[]{:S(2)}) collective-permute-start(f32[256,256]{0,1:T(8,128)S(1)} %add.121), channel_id=1, source_target_pairs={{0,8},{4,12},{8,0},{12,4},{1,9},{5,13},{9,1},{13,5},{2,10},{6,14},... | collective-permute-start | bytes 786440 | tf_op jit(solution)/shard_map/ppermute | solution.py:10
  118.0 11.0 %copy-start.4 = (bf16[256,1024]{1,0:T(8,128)(2,1)S(1)}, bf16[256,1024]{1,0:T(8,128)(2,1)}, u32[]{:S(2)}) copy-start(bf16[256,1024]{1,0:T(8,128)(2,1)} %copy-done.3) | copy-start | bytes 1572868
  119.3 7.4 %collective-permute-start.5 = (f32[256,256]{0,1:T(8,128)S(1)}, f32[256,256]{0,1:T(8,128)S(1)}, u32[]{:S(2)}, u32[]{:S(2)}) collective-permute-start(f32[256,256]{0,1:T(8,128)S(1)} %convolution_bitcast_fusion), channel_id=1, source_target_pairs={{0,4},{4,0},{8,12},{12,8},{1,5},{5,1},{9,13},{13,9},{2,6},{6,2},{1... | collective-permute-start | bytes 786440 | tf_op jit(solution)/shard_map/ppermute | solution.py:10
  138.0 60.0 %copy-start.1 = (bf16[1024,256]{1,0:T(8,128)(2,1)}, bf16[1024,256]{1,0:T(8,128)(2,1)S(1)}, u32[]{:S(2)}) copy-start(bf16[1024,256]{1,0:T(8,128)(2,1)S(1)} %scatter_custom_fusion.3) | copy-start | bytes 1572868
Sparse Core Ops, SparseCore 0:
  18.1 20.9 all-reduce.2
  41.4 24.3 all-reduce.4
  141.0 56.8 reduce-scatter.3
